TPU v7x, 32 devices: a whole 2x2x4 slice. The times are simulated.
32 devices in a mesh: patch: 8 (over z, x), tile: 4 (over y, core).
Axes of the slice: x: 2, y: 2, z: 4, core: 2. Of those that a mesh axis runs over, the one named last changes fastest.
Arguments:
- latents: float32 [1088, 128], P('patch')
- timestamps: int32 [1088], P('patch'), may hold values from 0 to 56, as said below
- cell_map: int32 [1024], replicated, may hold values from 0 to 1023, as said below
- w_video: bfloat16 [128, 3072], replicated, may hold values from -0.5 to 0.5
- w_audio: bfloat16 [128, 3072], replicated, may hold values from -0.5 to 0.5
- mod_scale: float32 [2, 3072], replicated, may hold values from -3 to 3
- mod_shift: float32 [2, 3072], replicated, may hold values from -3 to 3
- w_query: bfloat16 [3072, 3072], P(None, 'tile')
- w_key: bfloat16 [3072, 3072], P(None, 'tile')
- w_value: bfloat16 [3072, 3072], P(None, 'tile'), may hold values from -0.109375 to 0.109375
- q_gain: float32 [3072], P('tile'), as said below
- k_gain: float32 [3072], P('tile'), as said below
- k_cache: bfloat16 [1088, 3072], P('patch', 'tile'), may hold values from -8 to 8
- v_cache: bfloat16 [1088, 3072], P('patch', 'tile'), may hold values from -6 to 6
- w_out: bfloat16 [3072, 3072], P('tile'), may hold values from -0.109375 to 0.109375
- out_gain: float32 [3072], replicated, may hold values from 0.25 to 1.75
- w_final: bfloat16 [3072, 128], replicated, may hold values from -0.109375 to 0.109375
- step_sizes: float32 [2], replicated, may hold values from 0.2 to 0.6
- conv_w: bfloat16 [3, 3, 3, 128, 512], replicated, may hold values from -0.109375 to 0.109375
- conv_b: float32 [512], replicated, may hold values from -3 to 3
Outputs:
- final_latents: float32 [1088, 128], P('patch')
- decoded: bfloat16 [8, 16, 8, 512], P(None, 'patch', 'tile')
Inputs may be any that keep to these rules, and one draw needn't show every extreme that they name: `cell_map`: a permutation of the 1024 cells of the grid; entry r is the cell of the r-th video token, which stands in patch shard r // 128; cell (f, h, w) belongs to the decode block (h // 2, w // 2), held by patch index h // 2 and tile index w // 2; every patch shard holds exactly 4 cells of every decode block. A video token's timestamp is 8 times the frame of its cell; audio tokens' timestamps lie in the same span. `q_gain`: positive. `k_gain`: positive.
All inputs are finite; a program needn't handle non-finite values.
Results may differ from a plain program's by a relative error of at most 0.009.
Values may be sent and summed in bfloat16 or wider, within the bound.
A program may use at most 128 MiB of HBM per device.

v0:
```python
import jax
import jax.numpy as jnp
from jax import lax
from jax.sharding import PartitionSpec as P

HEAD = 128
VID_DEV = 128
STEPS = 2
FRAMES = 8
BH = 2


EPSILON = 1e-06


def with_halo(shard, sides, width):
    for axis, dim in sides:
        count, length = (lax.axis_size(axis), shard.shape[dim])
        up = [(i, (i + 1) % count) for i in range(count - 1)]
        down = [(j, i) for i, j in up]
        last = lax.slice_in_dim(shard, length - width, length, axis=dim)
        first = lax.slice_in_dim(shard, 0, width, axis=dim)
        before = lax.ppermute(last, axis, up)
        after = lax.ppermute(first, axis, down)
        shard = jnp.concatenate([before, shard, after], axis=dim)
    return shard


def row_scaled(matrix):
    return matrix * lax.rsqrt(jnp.mean(matrix * matrix, axis=-1, keepdims=True) + EPSILON)


def rotate(matrix, stamps):
    half_size = matrix.shape[-1] // 2
    frequency = jnp.exp(-jnp.log(10000.0) * jnp.arange(half_size, dtype=jnp.float32) / half_size)
    angles = stamps.astype(jnp.float32)[:, None, None] * frequency
    cosine = jnp.cos(angles)
    sines = jnp.sin(angles)
    leading = matrix[..., :half_size]
    trailing = matrix[..., half_size:]
    return jnp.concatenate(
        [leading * cosine - trailing * sines, leading * sines + trailing * cosine], axis=-1
    )


def head_project(normed, weight, gain, stamps):
    raw_out = jnp.dot(normed, weight, preferred_element_type=jnp.float32)
    shaped = raw_out.reshape(raw_out.shape[0], -1, HEAD)
    scaled = row_scaled(shaped) * gain.reshape(-1, HEAD)
    return rotate(scaled, stamps).reshape(raw_out.shape[0], -1).astype(jnp.bfloat16)


def attend_whole(queries, fresh_keys, values, stale_keys, stale_values, row_start):
    every_keys, every_values = (
        lax.all_gather(stale_keys, "patch", axis=0, tiled=True),
        lax.all_gather(stale_values, "patch", axis=0, tiled=True),
    )
    every_keys = lax.dynamic_update_slice_in_dim(every_keys, fresh_keys, row_start, 0)
    every_values = lax.dynamic_update_slice_in_dim(every_values, values, row_start, 0)
    row_count = queries.shape[0]
    query_heads = queries.reshape(row_count, -1, HEAD)
    key_heads = every_keys.reshape(every_keys.shape[0], -1, HEAD)
    value_heads = every_values.reshape(every_values.shape[0], -1, HEAD)
    scores = jnp.einsum(
        "qhd,khd->hqk", query_heads, key_heads, preferred_element_type=jnp.float32
    ) * HEAD ** (-0.5)
    row_top = jnp.max(scores, axis=2, keepdims=True)
    weights = jnp.exp(scores - row_top)
    totals = jnp.sum(weights, axis=2)
    result = jnp.einsum(
        "hqk,khd->qhd",
        weights.astype(jnp.bfloat16),
        value_heads,
        preferred_element_type=jnp.float32,
    )
    return (result / totals.T[:, :, None]).reshape(row_count, -1).astype(jnp.bfloat16)


def velocity_of(embedded, attended, w_out, out_gain, w_final):
    share_rows = attended.shape[0] // lax.axis_size("tile")
    own_rows = lax.dynamic_slice_in_dim(
        embedded, lax.axis_index("tile") * share_rows, share_rows, 0
    )
    mixed_rows = own_rows + lax.psum_scatter(
        jnp.dot(attended, w_out, preferred_element_type=jnp.float32).astype(jnp.bfloat16),
        "tile",
        scatter_dimension=0,
        tiled=True,
    ).astype(jnp.float32)
    final_normed = (row_scaled(mixed_rows) * out_gain).astype(jnp.bfloat16)
    own_velocity = jnp.dot(final_normed, w_final, preferred_element_type=jnp.float32)
    return lax.all_gather(own_velocity, "tile", axis=0, tiled=True)


def decode(latent_state, cell_map, conv_w, conv_b):
    video_rows = latent_state[:VID_DEV].astype(jnp.bfloat16)
    patch_count = lax.axis_size("patch")
    tile_count = lax.axis_size("tile")
    patch_index = lax.axis_index("patch")
    tile_index = lax.axis_index("tile")
    block_width = VID_DEV // (tile_count * FRAMES * BH)
    grid_rows = BH * patch_count
    grid_columns = block_width * tile_count
    cell_count = FRAMES * BH * block_width
    local_cells = jnp.arange(cell_count, dtype=jnp.int32)
    frame_ids = local_cells // (BH * block_width)
    inner_row = local_cells // block_width % BH
    inner_column = local_cells % block_width
    own_cells = (
        (frame_ids * grid_rows + patch_index * BH + inner_row) * grid_columns
        + tile_index * block_width
        + inner_column
    )
    matches = cell_map[None, :] == own_cells[:, None]
    every_video = lax.all_gather(video_rows, "patch", axis=0, tiled=True)
    sources = jnp.sum(
        jnp.where(matches, jnp.arange(cell_map.shape[0], dtype=jnp.int32)[None, :], 0), axis=1
    )
    block = every_video[sources]
    block = block.reshape(FRAMES, BH, block_width, -1)
    grown = with_halo(block, (("patch", 1), ("tile", 2)), 1)
    padded = jnp.pad(grown, ((1, 1), (0, 0), (0, 0), (0, 0)))
    columns = jnp.concatenate(
        [
            padded[
                shift_time : shift_time + FRAMES,
                shift_row : shift_row + BH,
                shift_column : shift_column + block_width,
            ]
            for shift_time in range(3)
            for shift_row in range(3)
            for shift_column in range(3)
        ],
        axis=-1,
    )
    kernel = conv_w.reshape(-1, conv_w.shape[-1])
    conv_out = (
        jnp.dot(columns.reshape(cell_count, -1), kernel, preferred_element_type=jnp.float32)
        + conv_b
    )
    return conv_out.astype(jnp.bfloat16).reshape(FRAMES, BH, block_width, -1)


def local(
    latents,
    timestamps,
    cell_map,
    w_video,
    w_audio,
    mod_scale,
    mod_shift,
    w_query,
    w_key,
    w_value,
    q_gain,
    k_gain,
    k_cache,
    v_cache,
    w_out,
    out_gain,
    w_final,
    step_sizes,
    conv_w,
    conv_b,
):
    row_count = latents.shape[0]
    row_start = lax.axis_index("patch") * row_count
    latent_state = latents
    stale_keys = k_cache
    stale_values = v_cache
    for step_index in range(STEPS):
        latent_b = latent_state.astype(jnp.bfloat16)
        video_part = jnp.dot(latent_b[:VID_DEV], w_video, preferred_element_type=jnp.float32)
        audio_part = jnp.dot(latent_b[VID_DEV:], w_audio, preferred_element_type=jnp.float32)
        embedded = jnp.concatenate([video_part, audio_part], axis=0)
        normed = (
            row_scaled(embedded) * (1.0 + mod_scale[step_index]) + mod_shift[step_index]
        ).astype(jnp.bfloat16)
        queries = head_project(normed, w_query, q_gain, timestamps)
        fresh_keys = head_project(normed, w_key, k_gain, timestamps)
        values = jnp.dot(normed, w_value, preferred_element_type=jnp.float32).astype(jnp.bfloat16)
        attended = attend_whole(queries, fresh_keys, values, stale_keys, stale_values, row_start)
        velocity = velocity_of(embedded, attended, w_out, out_gain, w_final)
        latent_state = latent_state - step_sizes[step_index] * velocity
        stale_keys = fresh_keys
        stale_values = values
    decoded = decode(latent_state, cell_map, conv_w, conv_b)
    return (latent_state, decoded)


def solution(mesh):
    return jax.shard_map(
        local,
        mesh=mesh,
        in_specs=(
            P("patch", None),
            P("patch"),
            P(),
            P(),
            P(),
            P(),
            P(),
            P(None, "tile"),
            P(None, "tile"),
            P(None, "tile"),
            P("tile"),
            P("tile"),
            P("patch", "tile"),
            P("patch", "tile"),
            P("tile", None),
            P(),
            P(),
            P(),
            P(),
            P(),
        ),
        out_specs=(P("patch", None), P(None, "patch", "tile", None)),
        check_vma=False,
    )
```

profile of v0, /device:TPU:0, one launch (start us, length us, event | category | flops | bytes accessed | tf_op | source)
XLA Modules:
  0.0 311.7 jit_solution(8176964901523891090)
XLA Ops:
  16.9 1.9 reshape.270
  18.8 1.9 multiply_reduce_fusion.4
  21.7 4.2 %fusion.94 = f32[136,768]{1,0:T(8,128)} fusion(bf16[136,3072]{1,0:T(8,128)(2,1)} %copy-done.7, bf16[3072,768]{1,0:T(8,128)(2,1)} %param.27), kind=kOutput, calls=%fused_computation.194 | convolution fusion | flops 641728512 | bytes 5971968 | tf_op jit(solution)/shard_map/dot_general | solution.py:47
  25.9 1.9 reshape.269
  27.9 1.9 multiply_reduce_fusion.5
  38.1 19.8 %all-gather.7.cloned.1.call-done = bf16[1088,768]{1,0:T(8,128)(2,1)} async-done(((bf16[136,768]{1,0:T(8,128)(2,1)}), bf16[1088,768]{1,0:T(8,128)(2,1)}) %all-gather.7.cloned.1.call-update) | async-done | bytes 1671184 | tf_op jit(solution)/shard_map/all_gather | solution.py:56
  58.0 4.2 %constant_dynamic-update-slice_fusion.28 = (bf16[1088,768]{1,0:T(8,128)(2,1)}, bf16[136,768]{1,0:T(8,128)(2,1)}) fusion(bf16[1088,768]{1,0:T(8,128)(2,1)} %all-gather.7.cloned.1.call-done, s32[]{:T(128)S(6)} %select_n.60, bf16[136,3072]{1,0:T(8,128)(2,1)} %copy-done.7, bf16[3072,768]{1,0:T(8,128)(2,1)} %param.29), kind=kOutput, calls=%fused_computation.161 | convolution fusion | flops 641832960 | bytes 5971972 | tf_op jit(solution)/shard_map/dot_general | solution.py:181
  62.2 3.8 %copy.84 = bf16[1088,768]{0,1:T(8,128)(2,1)} copy(bf16[1088,768]{1,0:T(8,128)(2,1)} %get-tuple-element.54) | data formatting | bytes 3342336 | tf_op jit(solution)/shard_map/dynamic_update_slice | solution.py:59
  66.0 38.1 %all-gather.9.cloned.1.call-done = bf16[1088,768]{1,0:T(8,128)(2,1)} async-done(((bf16[136,768]{1,0:T(8,128)(2,1)}), bf16[1088,768]{1,0:T(8,128)(2,1)}) %all-gather.9.cloned.1.call-update) | async-done | bytes 1671184 | tf_op jit(solution)/shard_map/all_gather | solution.py:55
  105.9 3.8 %copy.90 = bf16[1088,768]{0,1:T(8,128)(2,1)} copy(bf16[1088,768]{1,0:T(8,128)(2,1)} %constant_dynamic-update-slice_fusion.27) | data formatting | bytes 3342336 | tf_op jit(solution)/shard_map/dynamic_update_slice | solution.py:58
  109.7 2.7 fusion.92
  116.9 15.0 %fusion = bf16[40,3072]{1,0:T(8,128)(2,1)} fusion(bf16[136,3072]{1,0:T(8,128)(2,1)} %convolution_convert_fusion.1), kind=kCustom, calls=%all-reduce-scatter | all-reduce-scatter fusion | flops 491521 | bytes 1081856
  133.4 1.9 collective-permute-start.4
  136.1 5.4 %concatenate.139 = bf16[58,3072]{1,0:T(8,128)(2,1)} concatenate(bf16[18,3072]{1,0:T(8,128)(2,1)} %collective-permute-done.4, bf16[40,3072]{1,0:T(8,128)(2,1)} %fusion), dimensions={0} | concatenate | bytes 712704
  144.8 8.5 %all-gather = f32[4,34,128]{2,1,0:T(8,128)S(1)} all-gather(f32[1,34,128]{2,1,0:T(8,128)S(1)} %convolution_bitcast_fusion.1), channel_id=1, replica_groups=mesh['patch'=8,'tile'=4] {'tile'}, dimensions={0}, use_global_device_ids=true | all-gather | bytes 87040 | tf_op jit(solution)/shard_map/all_gather | solution.py:92
  162.8 4.0 %fusion.96 = f32[136,768]{1,0:T(8,128)} fusion(bf16[136,3072]{1,0:T(8,128)(2,1)S(1)} %add_convert_fusion, bf16[3072,768]{1,0:T(8,128)(2,1)} %param.27), kind=kOutput, calls=%fused_computation.196 | convolution fusion | flops 641728512 | bytes 5971968 | tf_op jit(solution)/shard_map/dot_general | solution.py:47
  168.7 1.9 multiply_reduce_fusion.3
  172.1 4.2 %fusion.97 = f32[136,768]{1,0:T(8,128)} fusion(bf16[136,3072]{1,0:T(8,128)(2,1)} %copy-done.8, bf16[3072,768]{1,0:T(8,128)(2,1)} %param.28), kind=kOutput, calls=%fused_computation.197 | convolution fusion | flops 641728512 | bytes 5971968 | tf_op jit(solution)/shard_map/dot_general | solution.py:47
  178.2 1.9 multiply_reduce_fusion.2
  188.7 3.8 %copy.100 = bf16[1088,768]{0,1:T(8,128)(2,1)} copy(bf16[1088,768]{1,0:T(8,128)(2,1)} %bitcast_dynamic-update-slice_fusion) | data formatting | bytes 3342336 | tf_op jit(solution)/shard_map/dynamic_update_slice | solution.py:58
  192.5 2.6 fusion.93
  198.2 4.1 %fusion.18 = bf16[1088,768]{1,0:T(8,128)(2,1)} fusion(bf16[1088,768]{1,0:T(8,128)(2,1)} %all-gather.11.cloned.1.call-done, s32[]{:T(128)S(6)} %select_n.60, bf16[136,3072]{1,0:T(8,128)(2,1)} %copy-done.8, bf16[3072,768]{1,0:T(8,128)(2,1)} %param.29), kind=kOutput, calls=%fused_computation.28 | convolution fusion | flops 641832960 | bytes 5763076 | tf_op jit(solution)/shard_map/dot_general | solution.py:181
  202.3 3.8 %copy.94 = bf16[1088,768]{0,1:T(8,128)(2,1)} copy(bf16[1088,768]{1,0:T(8,128)(2,1)} %fusion.18) | data formatting | bytes 3342336 | tf_op jit(solution)/shard_map/dynamic_update_slice | solution.py:59
  206.2 3.7 %fusion.34 = bf16[6,17,8,128]{3,2,1,0:T(8,128)(2,1)S(1)} fusion(bf16[1088,6,128]{0,2,1:T(8,128)(2,1)} %bitcast.154, f32[6,136,1088]{2,1,0:T(8,128)} %copy-done.6, f32[6,136]{1,0:T(8,128)} %copy-done.24, f32[136,6]{0,1:T(8,128)} %bitcast.194), kind=kOutput, calls=%fused_computation.35 | convolution fusion | flops 229263360 | bytes 5437824 | tf_op jit(solution)/shard_map/hqk,khd->qhd/dot_general | solution.py:70
  209.9 4.1 %convolution_convert_fusion = bf16[136,3072]{1,0:T(8,128)(2,1)} fusion(bf16[768,3072]{1,0:T(8,128)(2,1)} %param.34, bf16[6,17,8,128]{3,2,1,0:T(8,128)(2,1)S(1)} %fusion.34), kind=kOutput, calls=%fused_computation.5 | convolution fusion | flops 642146304 | bytes 5763072 | tf_op jit(solution)/shard_map/dot_general | solution.py:85
  214.0 15.9 %fusion.1 = bf16[40,3072]{1,0:T(8,128)(2,1)} fusion(bf16[136,3072]{1,0:T(8,128)(2,1)} %convolution_convert_fusion), kind=kCustom, calls=%all-reduce-scatter.1 | all-reduce-scatter fusion | flops 491521 | bytes 1081856
  230.9 1.9 collective-permute-start.5
  233.4 5.4 %concatenate.140 = bf16[58,3072]{1,0:T(8,128)(2,1)} concatenate(bf16[18,3072]{1,0:T(8,128)(2,1)} %collective-permute-done.5, bf16[40,3072]{1,0:T(8,128)(2,1)} %fusion.1), dimensions={0} | concatenate | bytes 712704
  242.2 8.5 %all-gather.1 = f32[4,34,128]{2,1,0:T(8,128)S(1)} all-gather(f32[1,34,128]{2,1,0:T(8,128)S(1)} %convolution_bitcast_fusion), channel_id=1, replica_groups=mesh['patch'=8,'tile'=4] {'tile'}, dimensions={0}, use_global_device_ids=true | all-gather | bytes 87040 | tf_op jit(solution)/shard_map/all_gather | solution.py:92
  255.0 32.8 %all_gather.27 = bf16[1024,128]{1,0:T(8,128)(2,1)} all-gather(bf16[128,128]{1,0:T(8,128)(2,1)S(1)} %slice.284), channel_id=1, replica_groups=mesh['patch'=8,'tile'=4] {'patch'}, dimensions={0}, use_global_device_ids=true | all-gather | bytes 294912 | tf_op jit(solution)/shard_map/all_gather | solution.py:115
  290.7 4.5 %collective-permute-start = (bf16[8,1,2,128]{3,2,1,0:T(2,128)(2,1)S(1)}, bf16[8,1,2,128]{3,2,1,0:T(2,128)(2,1)S(1)}, u32[]{:S(2)}, u32[]{:S(2)}) collective-permute-start(bf16[8,1,2,128]{3,2,1,0:T(2,128)(2,1)S(1)} %get-tuple-element.48), channel_id=1, source_target_pairs={{0,4},{4,8},{8,12},{12,16},{16,20},{20,24},{24,28},{1,5},{5,9},{9,... | collective-permute-start | bytes 12296 | tf_op jit(solution)/shard_map/ppermute | solution.py:23
  297.9 3.0 collective-permute-start.2
  (184 shorter events, 75.3 us)
Async XLA Ops:
  7.2 295.3 %copy-start = (bf16[3,3,3,128,512]{4,3,2,1,0:T(8,128)(2,1)S(1)}, bf16[3,3,3,128,512]{4,3,2,1,0:T(8,128)(2,1)}, u32[]{:S(2)}) copy-start(bf16[3,3,3,128,512]{4,3,2,1,0:T(8,128)(2,1)} %param.38) | copy-start | bytes 10616836
  7.2 50.8 %all-gather.7.cloned.1.call-start = ((), (), s32[]{:S(2)}) async-start(), calls=%async_computation | async-start | bytes 1880064 | tf_op jit(solution)/shard_map/all_gather | solution.py:56
  7.9 96.1 %all-gather.9.cloned.1.call-start = ((), (), s32[]{:S(2)}) async-start(), calls=%async_computation.1 | async-start | bytes 1880064 | tf_op jit(solution)/shard_map/all_gather | solution.py:55
  8.7 178.1 %all-gather.13.cloned.1.call-start = ((), (), s32[]{:S(2)}) async-start(), calls=%async_computation.3 | async-start | bytes 1880064 | tf_op jit(solution)/shard_map/all_gather | solution.py:55
  8.7 3.9 %copy-start.25 = (f32[2,3072]{1,0:T(2,128)S(1)}, f32[2,3072]{1,0:T(2,128)}, u32[]{:S(2)}) copy-start(f32[2,3072]{1,0:T(2,128)} %param.26) | copy-start | bytes 73732
  8.7 4.5 %copy-start.26 = (f32[2,3072]{1,0:T(2,128)S(1)}, f32[2,3072]{1,0:T(2,128)}, u32[]{:S(2)}) copy-start(f32[2,3072]{1,0:T(2,128)} %param.25) | copy-start | bytes 73732
  11.0 3.1 %copy-start.9 = (f32[8,3072]{1,0:T(8,128)}, f32[8,3072]{1,0:T(8,128)S(1)}, u32[]{:S(2)}) copy-start(f32[8,3072]{1,0:T(8,128)S(1)} %fusion.72) | copy-start | bytes 294916
  11.0 4.3 %copy-start.5 = (bf16[3072,768]{1,0:T(8,128)(2,1)S(1)}, bf16[3072,768]{1,0:T(8,128)(2,1)}, u32[]{:S(2)}) copy-start(bf16[3072,768]{1,0:T(8,128)(2,1)} %param.28) | copy-start | bytes 14155780
  31.8 2.7 copy-start.16
  31.8 2.7 copy-start.18
  33.3 2.8 copy-start.28
  33.3 3.6 %copy-start.31 = (u32[32]{0:T(128)S(1)}, u32[32]{0:T(128)}, u32[]{:S(2)}) copy-start(u32[32]{0:T(128)} %constant.105) | copy-start | bytes 388
  36.1 162.2 %all-gather.11.cloned.1.call-start = ((), (), s32[]{:S(2)}) async-start(), calls=%async_computation.2 | async-start | bytes 1880064 | tf_op jit(solution)/shard_map/all_gather | solution.py:56
  109.7 5.4 %slice-start = ((s8[4718592]{0:T(1024)(128)(4,1)}), s8[4194304]{0:T(1024)(128)(4,1)S(1)}, s32[]{:S(2)}) async-start(s8[4718592]{0:T(1024)(128)(4,1)} %bitcast.149), calls=%async_computation.4 | async-start | bytes 8388608
  112.4 2.7 slice-start.1
  115.1 20.3 %copy-start.30 = (f32[2]{0:T(128)S(1)}, f32[2]{0:T(128)}, u32[]{:S(2)}) copy-start(f32[2]{0:T(128)} %param.37) | copy-start | bytes 28
  131.8 11.3 %copy-start.21 = (f32[3072]{0:T(1024)S(1)}, f32[3072]{0:T(1024)}, u32[]{:S(2)}) copy-start(f32[3072]{0:T(1024)} %param.35) | copy-start | bytes 36868
  133.4 2.6 collective-permute-start.4
  159.1 1.8 copy-start.11
  159.1 1.8 copy-start.22
  159.1 1.8 copy-start.23
  172.1 11.0 %copy-start.27 = (f32[768]{0:T(1024)S(1)}, f32[768]{0:T(1024)}, u32[]{:S(2)}) copy-start(f32[768]{0:T(1024)} %param.30) | copy-start | bytes 9220
  181.7 3.8 %copy-start.17 = (f32[136,64]{1,0:T(8,128)S(1)}, f32[136,64]{1,0:T(8,128)}, u32[]{:S(2)}) copy-start(f32[136,64]{1,0:T(8,128)} %copy-done.16) | copy-start | bytes 104452
  181.7 3.8 %copy-start.19 = (f32[136,64]{1,0:T(8,128)S(1)}, f32[136,64]{1,0:T(8,128)}, u32[]{:S(2)}) copy-start(f32[136,64]{1,0:T(8,128)} %copy-done.18) | copy-start | bytes 104452
  195.1 1.8 copy-start.6
  195.1 1.8 copy-start.24
  230.9 2.6 collective-permute-start.5
  242.2 60.3 %copy-start.29 = (f32[512]{0:T(512)S(1)}, f32[512]{0:T(512)}, u32[]{:S(2)}) copy-start(f32[512]{0:T(512)} %param.39) | copy-start | bytes 6148
  289.4 5.9 %collective-permute-start.1 = (bf16[8,1,2,128]{3,2,1,0:T(2,128)(2,1)S(1)}, bf16[8,1,2,128]{3,2,1,0:T(2,128)(2,1)S(1)}, u32[]{:S(2)}, u32[]{:S(2)}) collective-permute-start(bf16[8,1,2,128]{3,2,1,0:T(2,128)(2,1)S(1)} %get-tuple-element.49), channel_id=1, source_target_pairs={{4,0},{8,4},{12,8},{16,12},{20,16},{24,20},{28,24},{5,1},{9,5},{13... | collective-permute-start | bytes 12296 | tf_op jit(solution)/shard_map/ppermute | solution.py:24
  290.7 5.9 %collective-permute-start = (bf16[8,1,2,128]{3,2,1,0:T(2,128)(2,1)S(1)}, bf16[8,1,2,128]{3,2,1,0:T(2,128)(2,1)S(1)}, u32[]{:S(2)}, u32[]{:S(2)}) collective-permute-start(bf16[8,1,2,128]{3,2,1,0:T(2,128)(2,1)S(1)} %get-tuple-element.48), channel_id=1, source_target_pairs={{0,4},{4,8},{8,12},{12,16},{16,20},{20,24},{24,28},{1,5},{5,9},{9,... | collective-permute-start | bytes 12296 | tf_op jit(solution)/shard_map/ppermute | solution.py:23
  296.6 4.3 %collective-permute-start.3 = (bf16[8,4,1,128]{3,2,1,0:T(2,128)(2,1)S(1)}, bf16[8,4,1,128]{3,2,1,0:T(2,128)(2,1)S(1)}, u32[]{:S(2)}, u32[]{:S(2)}) collective-permute-start(bf16[8,4,1,128]{3,2,1,0:T(2,128)(2,1)S(1)} %get-tuple-element.45), channel_id=1, source_target_pairs={{1,0},{2,1},{3,2},{5,4},{6,5},{7,6},{9,8},{10,9},{11,10},{13,12},{... | collective-permute-start | bytes 24584 | tf_op jit(solution)/shard_map/ppermute | solution.py:24
  297.9 3.9 %collective-permute-start.2 = (bf16[8,4,1,128]{3,2,1,0:T(2,128)(2,1)S(1)}, bf16[8,4,1,128]{3,2,1,0:T(2,128)(2,1)S(1)}, u32[]{:S(2)}, u32[]{:S(2)}) collective-permute-start(bf16[8,4,1,128]{3,2,1,0:T(2,128)(2,1)S(1)} %get-tuple-element.44), channel_id=1, source_target_pairs={{0,1},{1,2},{2,3},{4,5},{5,6},{6,7},{8,9},{9,10},{10,11},{12,13},{... | collective-permute-start | bytes 24584 | tf_op jit(solution)/shard_map/ppermute | solution.py:23
  (12 other events, 15.3 us)
Sparse Core Ops, SparseCore 0:
  10.2 47.7 all-gather.6
  60.1 43.8 all-gather.8
  106.2 43.8 all-gather.12
  152.2 43.8 all-gather.10
where the time goes:
time: 316 us; the launch traced here: 312 us
  blocking collectives  80.7 us (26%)
  waiting for transfers between devices  61.5 us (19%)
  local copies, waits for them, and re-layouts  56.3 us (18%)
  matrix products  48.8 us (15%)
  other arithmetic  35.3 us (11%)
  between operations  15 us (5%)
  starting transfers between devices  14.2 us (4%)
    all_gather x2, waiting for transfers between devices, attend_whole(): lax.all_gather(stale_keys, 'patch', axis=0, tiled=True)  38.1 us
    all_gather x1, blocking collectives, decode(): every_video = lax.all_gather(video_rows, 'patch', axis=0, tiled=True)  32.8 us
    unnamed x2, blocking collectives  30.9 us
    unnamed x99, local copies, waits for them, and re-layouts  21 us
    all_gather x2, waiting for transfers between devices, attend_whole(): lax.all_gather(stale_values, 'patch', axis=0, tiled=True)  19.9 us
    all_gather x2, blocking collectives, velocity_of(): return lax.all_gather(own_velocity, 'tile', axis=0, tiled=True)  17 us
    dot_general x4, matrix products, head_project(): raw_out = jnp.dot(normed, weight, preferred_element_type=jnp.float32)  14 us
    reduce_sum x8, other arithmetic, row_scaled(): jnp.mean(matrix * matrix, axis=-1, keepdims=True) + EPSILON  11.3 us
  transfers between devices with their start and end apart: 10, of which 4 were waited for; matrix products, arithmetic and copies ran while one was open for 37% of the time, Pallas kernels for 0%

commit v1 on v0

v1 whole, which is shorter than its diff:
```python
import functools

import jax
import jax.numpy as jnp
from jax import lax
from jax.experimental import pallas as pl
from jax.experimental.pallas import tpu as pltpu
from jax.sharding import PartitionSpec as P

HEAD = 128
VID_DEV = 128
STEPS = 2
FRAMES = 8
BH = 2
EPSILON = 1e-06
MESH = pl.DeviceIdType.MESH
F32 = jnp.float32
BF16 = jnp.bfloat16


def dot(a, b):
    return jnp.dot(a, b, preferred_element_type=F32)


def kernel(
    n,
    nt,
    latents,
    stamps,
    cells,
    mod_scale,
    mod_shift,
    q_gain,
    k_gain,
    k_cache,
    v_cache,
    out_gain,
    step_sizes,
    conv_b,
    wv_hbm,
    wa_hbm,
    wq_hbm,
    wk_hbm,
    wval_hbm,
    wo_hbm,
    wf_hbm,
    cw_hbm,
    state_out,
    conv_out,
    w_vid,
    w_aud,
    w_q,
    w_k,
    w_val,
    w_o,
    w_f,
    kv,
    emb,
    normed,
    q_ref,
    att,
    cos_ref,
    sin_ref,
    acc,
    s1_send,
    s1_recv,
    s2_send,
    s2_recv,
    vel_send,
    vel_recv,
    vid,
    onehot,
    grown,
    load_sem,
    ring_send,
    ring_recv,
    s1_ss,
    s1_rs,
    s2_ss,
    s2_rs,
    v_ss,
    v_rs,
    vid_ss,
    vid_rs,
):
    rows = latents.shape[0]
    pad = kv.shape[4]
    width = emb.shape[1]
    cols = q_ref.shape[1]
    half = cols // 2
    quarter = width // nt
    me = lax.axis_index("patch")
    tile = lax.axis_index("tile")
    core = tile % 2
    ty = tile // 2
    ny = nt // 2

    loads = []
    for i, (src, dst) in enumerate(
        (
            (wv_hbm, w_vid),
            (wa_hbm, w_aud),
            (wk_hbm, w_k),
            (wval_hbm, w_val),
            (wq_hbm, w_q),
            (wo_hbm, w_o),
            (wf_hbm, w_f),
        )
    ):
        copy = pltpu.make_async_copy(src, dst, load_sem.at[i])
        copy.start()
        loads.append(copy)

    barrier = pltpu.get_barrier_semaphore()
    for j in range(1, n):
        pl.semaphore_signal(
            barrier, inc=1, device_id=(lax.rem(me + j, n), tile), device_id_type=MESH
        )
    for j in range(1, nt):
        pl.semaphore_signal(
            barrier, inc=1, device_id=(me, lax.rem(tile + j, nt)), device_id_type=MESH
        )

    for d in range(2):
        for w, src in enumerate((k_cache, v_cache)):
            block = src[:, d * half : (d + 1) * half].astype(F32)
            block = jnp.concatenate([block, jnp.zeros((pad - rows, half), F32)], axis=0)
            kv[1, d, 0, w] = block.astype(BF16)
    pl.semaphore_wait(barrier, n - 1 + nt - 1)

    odd = me % 2
    pos = (1 - odd) * (me // 2) + odd * (n - 1 - me // 2)

    def at_pos(p):
        p = lax.rem(p + n, n)
        back = p // (n // 2)
        return (1 - back) * (2 * p) + back * (2 * (n - 1 - p) + 1)

    nexts = (at_pos(pos + 1), at_pos(pos - 1))

    def hop(step, s, d):
        if s > 0:
            src = kv.at[step, d, s]
        elif step == 0:
            src = kv.at[1, d, 0]
        else:
            src = kv.at[step - 1, d, 0]
        return pltpu.make_async_remote_copy(
            src_ref=src,
            dst_ref=kv.at[step, d, s + 1],
            send_sem=ring_send.at[step, d, s],
            recv_sem=ring_recv.at[step, d, s],
            device_id=(nexts[d], tile),
            device_id_type=MESH,
        )

    queue = [(step, s) for step in range(STEPS) for s in range(n - 1)]
    done = [0]

    def start_hop(index):
        for d in range(2):
            hop(*queue[index], d).start()

    def service(limit=None):
        i = done[0]
        if i >= len(queue) or (limit is not None and queue[i][0] > limit):
            return
        for d in range(2):
            hop(*queue[i], d).wait_recv()
            if i + 1 < len(queue):
                hop(*queue[i + 1], d).start()
        done[0] = i + 1

    start_hop(0)

    lane = lax.broadcasted_iota(jnp.int32, (1, HEAD), 1)
    frequency = jnp.exp(-jnp.log(F32(10000.0)) * (lane % (HEAD // 2)).astype(F32) / (HEAD // 2))
    angles = stamps[...].astype(F32) * frequency
    cos_ref[...] = jnp.cos(angles)
    sin_ref[...] = jnp.where(lane < HEAD // 2, -1.0, 1.0) * jnp.sin(angles)

    bw = VID_DEV // (nt * FRAMES * BH)
    gw = bw + 2
    slots = 2 * FRAMES
    row = lax.broadcasted_iota(jnp.int32, (onehot.shape[0], 1), 0)
    f_id = row % slots - 1
    h_id = row // (slots * gw) - 1 + me * BH
    w_id = row // slots % gw - 1 + tile * bw
    inside = (
        (f_id >= 0)
        & (f_id < FRAMES)
        & (h_id >= 0)
        & (h_id < n * BH)
        & (w_id >= 0)
        & (w_id < nt * bw)
    )
    wanted = jnp.where(inside, (f_id * (n * BH) + h_id) * (nt * bw) + w_id, -1)
    for j in range(n):
        c = slice(j * VID_DEV, (j + 1) * VID_DEV)
        onehot[:, c] = jnp.where(cells[:, c] == wanted, 1.0, 0.0).astype(BF16)

    state_out[...] = latents[...]
    waited = set()

    def need(i):
        if i not in waited:
            loads[i].wait()
            waited.add(i)

    chunk = 256

    def project(weight, gain, put):
        @pl.loop(0, cols // chunk)
        def _(i):
            cs = pl.ds(pl.multiple_of(i * chunk, chunk), chunk)
            raw = dot(normed[...], weight[:, cs])
            for h in range(chunk // HEAD):
                hs = pl.ds(pl.multiple_of(i * chunk + h * HEAD, HEAD), HEAD)
                x = raw[:, h * HEAD : (h + 1) * HEAD]
                if gain is not None:
                    x = x * lax.rsqrt(jnp.mean(x * x, axis=1, keepdims=True) + EPSILON)
                    x = x * gain[:, hs]
                    x = x * cos_ref[...] + pltpu.roll(x, HEAD // 2, 1) * sin_ref[...]
                put(i * (chunk // HEAD) + h, hs, x)

    heads_half = half // HEAD

    for step in range(STEPS):
        need(0)
        need(1)
        state = state_out[...]
        vid_b = state[:VID_DEV].astype(BF16)
        aud_b = state[VID_DEV:].astype(BF16)
        square = jnp.zeros((rows, 1), F32)
        wide = width // 4
        for i in range(4):
            c = slice(i * wide, (i + 1) * wide)
            e = jnp.concatenate([dot(vid_b, w_vid[:, c]), dot(aud_b, w_aud[:, c])], axis=0)
            emb[:, c] = e
            square = square + jnp.sum(e * e, axis=1, keepdims=True)
        scale = lax.rsqrt(square / width + EPSILON)
        for i in range(4):
            c = slice(i * wide, (i + 1) * wide)
            x = emb[:, c] * scale * (1.0 + mod_scale[step : step + 1, c])
            normed[:, c] = (x + mod_shift[step : step + 1, c]).astype(BF16)
        service()

        def put_kv(which):
            def put(h, hs, x):
                x = jnp.concatenate([x, jnp.zeros((pad - rows, HEAD), F32)], axis=0)
                d = h // heads_half
                cs = pl.ds(pl.multiple_of((h % heads_half) * HEAD, HEAD), HEAD)
                kv[step, d, 0, which, :, cs] = x.astype(BF16)

            return put

        def put_q(h, hs, x):
            q_ref[:, hs] = x.astype(BF16)

        need(2)
        if step == 1:
            for d in range(2):
                hop(0, 0, d).wait_send()
        project(w_k, k_gain, put_kv(0))
        service()
        need(3)
        project(w_val, None, put_kv(1))
        service()
        need(4)
        project(w_q, q_gain, put_q)
        if step == STEPS - 1:
            taps = cw_hbm.shape[0]
            out_ch = cw_hbm.shape[1]
            conv_loads = [
                pltpu.make_async_copy(
                    cw_hbm.at[0:width], w_q.at[:, 0:out_ch], load_sem.at[7]
                ),
                pltpu.make_async_copy(
                    cw_hbm.at[width:taps], w_k.at[0 : taps - width, 0:out_ch], load_sem.at[8]
                ),
            ]
            for copy in conv_loads:
                copy.start()
        while done[0] < (step + 1) * (n - 1):
            service()

        for d in range(2):

            @pl.loop(0, heads_half)
            def _(h, d=d):
                hs = pl.ds(pl.multiple_of(h * HEAD, HEAD), HEAD)
                qs = pl.ds(pl.multiple_of(d * half + h * HEAD, HEAD), HEAD)
                keys = kv[step, d, :, 0, :, hs].reshape(n * pad, HEAD)
                values = kv[step, d, :, 1, :, hs].reshape(n * pad, HEAD)
                scores = lax.dot_general(
                    q_ref[:, qs], keys, (((1,), (1,)), ((), ())), preferred_element_type=F32
                )
                key_id = lax.broadcasted_iota(jnp.int32, (1, n * pad), 1)
                scores = jnp.where(key_id % pad < rows, scores, -jnp.inf)
                top = jnp.max(scores, axis=1, keepdims=True)
                weights = jnp.exp((scores - top) * HEAD ** (-0.5))
                total = jnp.sum(weights, axis=1, keepdims=True)
                att[:, qs] = (dot(weights.astype(BF16), values) / total).astype(BF16)

            service()

        need(5)

        def out_part(owner):
            cs = pl.ds(pl.multiple_of(owner * quarter, HEAD), quarter)
            return dot(att[...], w_o[:, cs])

        def pad_rows(x):
            return jnp.concatenate([x, jnp.zeros((pad - rows, x.shape[1]), F32)], axis=0)

        def tile_copy(src, dst, ss, rs, target):
            return pltpu.make_async_remote_copy(
                src_ref=src,
                dst_ref=dst,
                send_sem=ss,
                recv_sem=rs,
                device_id=(me, target),
                device_id_type=MESH,
            )

        sibling = ty * 2 + 1 - core
        first = []
        for j in list(range(1, ny)) + [0]:
            chip = lax.rem(ty + j, ny)
            s1_send[j] = pad_rows(out_part(chip * 2 + 1 - core)).astype(BF16)
            copy = tile_copy(
                s1_send.at[j], s1_recv.at[j], s1_ss.at[step, j], s1_rs.at[step, j], sibling
            )
            copy.start()
            first.append((j, copy))
        second = []
        for j, copy in first:
            chip = lax.rem(ty + j, ny)
            mine = out_part(chip * 2 + core)
            copy.wait_recv()
            mine = mine + s1_recv[j].astype(F32)[:rows]
            if j > 0:
                s2_send[j - 1] = pad_rows(mine).astype(BF16)
                far = tile_copy(
                    s2_send.at[j - 1],
                    s2_recv.at[j - 1],
                    s2_ss.at[step, j],
                    s2_rs.at[step, j],
                    chip * 2 + core,
                )
                far.start()
                second.append((j, far))
            else:
                es = pl.ds(pl.multiple_of(tile * quarter, HEAD), quarter)
                acc[...] = mine + emb[:, es]
        service()
        for j, far in second:
            far.wait_recv()
            acc[...] += s2_recv[j - 1].astype(F32)[:rows]
        need(6)
        mixed = acc[...]
        es = pl.ds(pl.multiple_of(tile * quarter, HEAD), quarter)
        square = jnp.sum(mixed * mixed, axis=1, keepdims=True)
        part = dot((mixed * out_gain[:, es]).astype(BF16), w_f[es, :])
        vel_send[0] = jnp.concatenate(
            [part, jnp.broadcast_to(square, (rows, HEAD))], axis=1
        )
        near = tile_copy(
            vel_send.at[0], vel_recv.at[0], v_ss.at[step, 0], v_rs.at[step, 0], sibling
        )
        near.start()
        near.wait_recv()
        both = vel_send[0] + vel_recv[0]
        vel_send[1] = both
        others = []
        for j in range(1, ny):
            copy = tile_copy(
                vel_send.at[1],
                vel_recv.at[j],
                v_ss.at[step, j],
                v_rs.at[step, j],
                lax.rem(ty + j, ny) * 2 + core,
            )
            copy.start()
            others.append(copy)
        service()
        for j, copy in enumerate(others):
            copy.wait_recv()
            both = both + vel_recv[j + 1]
        channels = part.shape[1]
        scale = lax.rsqrt(both[:, channels : channels + 1] / width + EPSILON)
        state_out[...] = state - step_sizes[step] * (both[:, :channels] * scale)
        for _, copy in first:
            copy.wait_send()
        for _, copy in second:
            copy.wait_send()
        near.wait_send()
        for copy in others:
            copy.wait_send()

    vid[me] = state_out[:VID_DEV, :].astype(BF16)
    sends = []
    for j in list(range(1, n)):
        copy = pltpu.make_async_remote_copy(
            src_ref=vid.at[me],
            dst_ref=vid.at[me],
            send_sem=vid_ss.at[j],
            recv_sem=vid_rs.at[j],
            device_id=(lax.rem(me + j, n), tile),
            device_id_type=MESH,
        )
        copy.start()
        sends.append(copy)
    for index in range(1, len(queue)):
        for d in range(2):
            hop(*queue[index], d).wait_send()
    for copy in conv_loads:
        copy.wait()
    for j in range(1, n):
        source = lax.rem(me - j + n, n)
        pltpu.make_async_remote_copy(
            src_ref=vid.at[source],
            dst_ref=vid.at[source],
            send_sem=vid_ss.at[j],
            recv_sem=vid_rs.at[j],
            device_id=(source, tile),
            device_id_type=MESH,
        ).wait_recv()
    grown[...] = dot(onehot[...], vid[...].reshape(n * VID_DEV, HEAD))
    pieces = []
    for a in range(3):
        for b in range(3):
            for c in range(3):
                starts = [
                    ((h + b) * gw + w + c) * slots + a for h in range(BH) for w in range(bw)
                ]
                pieces.append(
                    jnp.concatenate([grown[s : s + FRAMES, :] for s in starts], axis=0).astype(BF16)
                )
    cut = width // HEAD
    total = dot(jnp.concatenate(pieces[:cut], axis=1), w_q[:, 0:out_ch])
    total = total + dot(jnp.concatenate(pieces[cut:], axis=1), w_k[0 : taps - width, 0:out_ch])
    conv_out[...] = (total + conv_b[...]).astype(BF16)
    for copy in sends:
        copy.wait_send()


def local(
    latents,
    timestamps,
    cell_map,
    w_video,
    w_audio,
    mod_scale,
    mod_shift,
    w_query,
    w_key,
    w_value,
    q_gain,
    k_gain,
    k_cache,
    v_cache,
    w_out,
    out_gain,
    w_final,
    step_sizes,
    conv_w,
    conv_b,
):
    n, nt = lax.axis_size("patch"), lax.axis_size("tile")
    rows, channels = latents.shape
    width = w_query.shape[0]
    cols = w_query.shape[1]
    pad = -(-rows // 16) * 16
    quarter = width // nt
    ny = nt // 2
    bw = VID_DEV // (nt * FRAMES * BH)
    border = (BH + 2) * (bw + 2) * 2 * FRAMES
    cells = FRAMES * BH * bw
    out_ch = conv_w.shape[-1]
    conv_flat = conv_w.reshape(-1, out_ch)
    vmem = pl.BlockSpec(memory_space=pltpu.VMEM)
    hbm = pl.BlockSpec(memory_space=pl.ANY)
    dma = pltpu.SemaphoreType.DMA
    state, conv = pl.pallas_call(
        functools.partial(kernel, n, nt),
        out_shape=(
            jax.ShapeDtypeStruct((rows, channels), F32),
            jax.ShapeDtypeStruct((cells, out_ch), BF16),
        ),
        in_specs=[vmem] * 10 + [pl.BlockSpec(memory_space=pltpu.SMEM), vmem] + [hbm] * 8,
        out_specs=(vmem, vmem),
        scratch_shapes=[
            pltpu.VMEM(w_video.shape, BF16),
            pltpu.VMEM(w_audio.shape, BF16),
            pltpu.VMEM(w_query.shape, BF16),
            pltpu.VMEM(w_key.shape, BF16),
            pltpu.VMEM(w_value.shape, BF16),
            pltpu.VMEM(w_out.shape, BF16),
            pltpu.VMEM(w_final.shape, BF16),
            pltpu.VMEM((STEPS, 2, n, 2, pad, cols // 2), BF16),
            pltpu.VMEM((rows, width), F32),
            pltpu.VMEM((rows, width), BF16),
            pltpu.VMEM((rows, cols), BF16),
            pltpu.VMEM((rows, cols), BF16),
            pltpu.VMEM((rows, HEAD), F32),
            pltpu.VMEM((rows, HEAD), F32),
            pltpu.VMEM((rows, quarter), F32),
            pltpu.VMEM((ny, pad, quarter), BF16),
            pltpu.VMEM((ny, pad, quarter), BF16),
            pltpu.VMEM((ny - 1, pad, quarter), BF16),
            pltpu.VMEM((ny - 1, pad, quarter), BF16),
            pltpu.VMEM((2, rows, channels + HEAD), F32),
            pltpu.VMEM((ny, rows, channels + HEAD), F32),
            pltpu.VMEM((n, VID_DEV, channels), BF16),
            pltpu.VMEM((border, n * VID_DEV), BF16),
            pltpu.VMEM((border, channels), F32),
            dma((9,)),
            dma((STEPS, 2, n - 1)),
            dma((STEPS, 2, n - 1)),
            dma((STEPS, ny)),
            dma((STEPS, ny)),
            dma((STEPS, ny)),
            dma((STEPS, ny)),
            dma((STEPS, ny)),
            dma((STEPS, ny)),
            dma((n,)),
            dma((n,)),
        ],
        compiler_params=pltpu.CompilerParams(
            collective_id=0, has_side_effects=True, vmem_limit_bytes=63 * 1024 * 1024
        ),
    )(
        latents,
        timestamps.reshape(-1, 1),
        cell_map.reshape(1, -1),
        mod_scale,
        mod_shift,
        q_gain.reshape(1, -1),
        k_gain.reshape(1, -1),
        k_cache,
        v_cache,
        out_gain.reshape(1, -1),
        step_sizes,
        conv_b.reshape(1, -1),
        w_video,
        w_audio,
        w_query,
        w_key,
        w_value,
        w_out,
        w_final,
        conv_flat,
    )
    decoded = conv.reshape(BH, bw, FRAMES, out_ch).transpose(2, 0, 1, 3)
    return state, decoded


def solution(mesh):
    return jax.shard_map(
        local,
        mesh=mesh,
        in_specs=(
            P("patch", None),
            P("patch"),
            P(),
            P(),
            P(),
            P(),
            P(),
            P(None, "tile"),
            P(None, "tile"),
            P(None, "tile"),
            P("tile"),
            P("tile"),
            P("patch", "tile"),
            P("patch", "tile"),
            P("tile", None),
            P(),
            P(),
            P(),
            P(),
            P(),
        ),
        out_specs=(P("patch", None), P(None, "patch", "tile", None)),
        check_vma=False,
    )
```

time: 316 us -> 129 us (0.41); the launches traced: 312 us -> 128 us
  Pallas kernels: 0 us -> 121 us
  blocking collectives: 80.7 us -> 0 us
  waiting for transfers between devices: 61.5 us -> 0 us
  local copies, waits for them, and re-layouts: 56.3 us -> 6.87 us
  matrix products: 48.8 us -> 0 us
  other arithmetic: 35.3 us -> 0 us
  between operations: 15 us -> 0.64 us
  starting transfers between devices: 14.2 us -> 0 us
    pallas_call x0 -> x1, Pallas kernels: none -> 121 us  [local(): pl.pallas_call(functools.partial(kernel, n, nt), out_shape=(jax.ShapeDtyp...]
    all_gather x4 -> x0, waiting for transfers between devices: 57.9 us -> none  [the longest x2 38.1 us: attend_whole(): lax.all_gather(stale_keys, 'patch', axis=0, tiled=True)]
    all_gather x3 -> x0, blocking collectives: 49.8 us -> none  [the longest x1 32.8 us: decode(): every_video = lax.all_gather(video_rows, 'patch', axis=0, tiled=True)]
    dot_general x19 -> x0, matrix products: 48.8 us -> none  [the longest x4 14 us: head_project(): raw_out = jnp.dot(normed, weight, preferred_element_type=jnp.float32)]
    unnamed x2 -> x0, blocking collectives: 30.9 us -> none
    unnamed x99 -> x1, local copies, waits for them, and re-layouts: 21 us -> 1.52 us
    dynamic_update_slice x4 -> x0, local copies, waits for them, and re-layouts: 15.3 us -> none  [the longest x2 7.66 us: attend_whole(): lax.dynamic_update_slice_in_dim(every_values, values, row_start, 0)]
    reduce_sum x11 -> x0, other arithmetic: 13.5 us -> none  [the longest x8 11.3 us: row_scaled(): jnp.mean(matrix * matrix, axis=-1, keepdims=True) + EPSILON]
  transfers between devices with their start and end apart: 10 -> 0, of which waited for: 4 -> 0; matrix products, arithmetic and copies ran while one was open for 37% -> 0% of each run, Pallas kernels for 0% -> 0%
where the time goes in v1:
time: 129 us; the launch traced here: 128 us
  Pallas kernels  121 us (94%)
  local copies, waits for them, and re-layouts  6.87 us (5%)
    pallas_call x1, Pallas kernels, local(): pl.pallas_call(functools.partial(kernel, n, nt), out_shape=(jax.ShapeDtyp...  121 us

profile of v1, /device:TPU:0, one launch (start us, length us, event | category | flops | bytes accessed | tf_op | source)
XLA Modules:
  0.0 128.3 jit_solution(5460261325375974039)
XLA Ops:
  0.6 1.3 reshape.30.q_gain
  1.9 1.3 reshape.31.k_gain
  3.2 1.4 %copy.23.stamps = s32[136,1]{1,0:T(8,128)} copy(s32[136,1]{0,1:T(1,128)} %bitcast.15) | data formatting | bytes 1088 | tf_op jit(solution)/shard_map/reshape | solution.py:535
  4.6 120.8 %shard_map.203 = (f32[136,128]{1,0:T(8,128)}, bf16[32,512]{1,0:T(8,128)(2,1)}) custom-call(f32[136,128]{1,0:T(8,128)} %latents.1, s32[136,1]{1,0:T(8,128)} %copy.23.stamps, s32[1,1024]{1,0:T(1,128)} %bitcast.13, f32[2,3072]{1,0:T(2,128)} %mod_scale.1, f32[2,3072]{1,0:T(2,128)} %mod_shift.1, f32[1,768]{1,0:T(1,128)} %reshape.30.q_gain, ...), custom_call_target="tpu_custom_call" | custom-call | tf_op jit(solution)/shard_map/pallas_call | solution.py:485
  125.4 1.4 %copy.26 = bf16[2,2,8,512]{3,1,0,2:T(2,128)(2,1)} copy(bf16[2,2,8,512]{3,2,1,0:T(8,128)(2,1)} %bitcast.11) | data formatting | bytes 65536 | tf_op jit(solution)/shard_map/reshape | solution.py:555
  126.8 1.5 %copy.28 = f32[136,128]{1,0:T(8,128)} copy(f32[136,128]{1,0:T(8,128)} %get-tuple-element.8) | data formatting | bytes 139264

commit v2 on v1

--- a/solution.py
+++ b/solution.py
@@ -138,23 +138,23 @@
 
     nexts = (at_pos(pos + 1), at_pos(pos - 1))
 
-    def hop(step, s, d):
+    def hop(step, s, w, d):
         if s > 0:
-            src = kv.at[step, d, s]
+            src = kv.at[step, d, s, w]
         elif step == 0:
-            src = kv.at[1, d, 0]
+            src = kv.at[1, d, 0, w]
         else:
-            src = kv.at[step - 1, d, 0]
+            src = kv.at[step - 1, d, 0, w]
         return pltpu.make_async_remote_copy(
             src_ref=src,
-            dst_ref=kv.at[step, d, s + 1],
-            send_sem=ring_send.at[step, d, s],
-            recv_sem=ring_recv.at[step, d, s],
+            dst_ref=kv.at[step, d, s + 1, w],
+            send_sem=ring_send.at[step, d, s, w],
+            recv_sem=ring_recv.at[step, d, s, w],
             device_id=(nexts[d], tile),
             device_id_type=MESH,
         )
 
-    queue = [(step, s) for step in range(STEPS) for s in range(n - 1)]
+    queue = [(step, s, w) for step in range(STEPS) for s in range(n - 1) for w in range(2)]
     done = [0]
 
     def start_hop(index):
@@ -167,15 +167,19 @@
             return
         for d in range(2):
             hop(*queue[i], d).wait_recv()
-            if i + 1 < len(queue):
-                hop(*queue[i + 1], d).start()
+            if i + 2 < len(queue):
+                hop(*queue[i + 2], d).start()
         done[0] = i + 1
 
     start_hop(0)
+    start_hop(1)
 
     lane = lax.broadcasted_iota(jnp.int32, (1, HEAD), 1)
     frequency = jnp.exp(-jnp.log(F32(10000.0)) * (lane % (HEAD // 2)).astype(F32) / (HEAD // 2))
-    angles = stamps[...].astype(F32) * frequency
+    here = lax.broadcasted_iota(jnp.int32, (rows, rows), 0)
+    there = lax.broadcasted_iota(jnp.int32, (rows, rows), 1)
+    times = jnp.where(here == there, stamps[...].astype(F32), 0.0)
+    angles = jnp.sum(times, axis=1, keepdims=True) * frequency
     cos_ref[...] = jnp.cos(angles)
     sin_ref[...] = jnp.where(lane < HEAD // 2, -1.0, 1.0) * jnp.sin(angles)
 
@@ -219,7 +223,7 @@
                 x = raw[:, h * HEAD : (h + 1) * HEAD]
                 if gain is not None:
                     x = x * lax.rsqrt(jnp.mean(x * x, axis=1, keepdims=True) + EPSILON)
-                    x = x * gain[:, hs]
+                    x = x * gain[pl.ds(i * (chunk // HEAD) + h, 1), :]
                     x = x * cos_ref[...] + pltpu.roll(x, HEAD // 2, 1) * sin_ref[...]
                 put(i * (chunk // HEAD) + h, hs, x)
 
@@ -243,7 +247,8 @@
             c = slice(i * wide, (i + 1) * wide)
             x = emb[:, c] * scale * (1.0 + mod_scale[step : step + 1, c])
             normed[:, c] = (x + mod_shift[step : step + 1, c]).astype(BF16)
-        service()
+        service(step)
+        service(step)
 
         def put_kv(which):
             def put(h, hs, x):
@@ -260,12 +265,15 @@
         need(2)
         if step == 1:
             for d in range(2):
-                hop(0, 0, d).wait_send()
+                for w in range(2):
+                    hop(0, 0, w, d).wait_send()
         project(w_k, k_gain, put_kv(0))
-        service()
+        service(step)
+        service(step)
         need(3)
         project(w_val, None, put_kv(1))
-        service()
+        service(step)
+        service(step)
         need(4)
         project(w_q, q_gain, put_q)
         if step == STEPS - 1:
@@ -281,15 +289,14 @@
             ]
             for copy in conv_loads:
                 copy.start()
-        while done[0] < (step + 1) * (n - 1):
+        while done[0] < (step + 1) * 2 * (n - 1):
             service()
 
         for d in range(2):
 
-            @pl.loop(0, heads_half)
-            def _(h, d=d):
-                hs = pl.ds(pl.multiple_of(h * HEAD, HEAD), HEAD)
-                qs = pl.ds(pl.multiple_of(d * half + h * HEAD, HEAD), HEAD)
+            for h in range(heads_half):
+                hs = slice(h * HEAD, (h + 1) * HEAD)
+                qs = slice(d * half + h * HEAD, d * half + (h + 1) * HEAD)
                 keys = kv[step, d, :, 0, :, hs].reshape(n * pad, HEAD)
                 values = kv[step, d, :, 1, :, hs].reshape(n * pad, HEAD)
                 scores = lax.dot_general(
@@ -301,8 +308,7 @@
                 weights = jnp.exp((scores - top) * HEAD ** (-0.5))
                 total = jnp.sum(weights, axis=1, keepdims=True)
                 att[:, qs] = (dot(weights.astype(BF16), values) / total).astype(BF16)
-
-            service()
+                service()
 
         need(5)
 
@@ -333,10 +339,12 @@
             )
             copy.start()
             first.append((j, copy))
+            service()
         second = []
         for j, copy in first:
             chip = lax.rem(ty + j, ny)
             mine = out_part(chip * 2 + core)
+            service()
             copy.wait_recv()
             mine = mine + s1_recv[j].astype(F32)[:rows]
             if j > 0:
@@ -369,6 +377,7 @@
             vel_send.at[0], vel_recv.at[0], v_ss.at[step, 0], v_rs.at[step, 0], sibling
         )
         near.start()
+        service()
         near.wait_recv()
         both = vel_send[0] + vel_recv[0]
         vel_send[1] = both
@@ -411,7 +420,7 @@
         )
         copy.start()
         sends.append(copy)
-    for index in range(1, len(queue)):
+    for index in range(2, len(queue)):
         for d in range(2):
             hop(*queue[index], d).wait_send()
     for copy in conv_loads:
@@ -516,8 +525,8 @@
             pltpu.VMEM((border, n * VID_DEV), BF16),
             pltpu.VMEM((border, channels), F32),
             dma((9,)),
-            dma((STEPS, 2, n - 1)),
-            dma((STEPS, 2, n - 1)),
+            dma((STEPS, 2, n - 1, 2)),
+            dma((STEPS, 2, n - 1, 2)),
             dma((STEPS, ny)),
             dma((STEPS, ny)),
             dma((STEPS, ny)),
@@ -532,12 +541,12 @@
         ),
     )(
         latents,
-        timestamps.reshape(-1, 1),
+        timestamps.reshape(1, -1),
         cell_map.reshape(1, -1),
         mod_scale,
         mod_shift,
-        q_gain.reshape(1, -1),
-        k_gain.reshape(1, -1),
+        q_gain.reshape(-1, HEAD),
+        k_gain.reshape(-1, HEAD),
         k_cache,
         v_cache,
         out_gain.reshape(1, -1),

time: 129 us -> 113 us (0.88)
  Pallas kernels: 121 us -> 109 us
  local copies, waits for them, and re-layouts: 6.87 us -> 2.92 us
    pallas_call x1, Pallas kernels: 121 us -> 109 us  [local(): pl.pallas_call(functools.partial(kernel, n, nt), out_shape=(jax.ShapeDtyp...]
    reshape x3 -> x0, local copies, waits for them, and re-layouts: 3.96 us -> none  [the longest x1 1.42 us: local(): timestamps.reshape(-1, 1)]
where the time goes in v2:
time: 113 us
  Pallas kernels  109 us (96%)
  local copies, waits for them, and re-layouts  2.92 us (3%)
    pallas_call x1, Pallas kernels, local(): pl.pallas_call(functools.partial(kernel, n, nt), out_shape=(jax.ShapeDtyp...  109 us

profile of v2, /device:TPU:0, one launch (start us, length us, event | category | flops | bytes accessed | tf_op | source)
XLA Modules:
  0.0 112.8 jit_solution(8788970441785093094)
XLA Ops:
  0.6 109.3 %shard_map.203 = (f32[136,128]{1,0:T(8,128)}, bf16[32,512]{1,0:T(8,128)(2,1)}) custom-call(f32[136,128]{1,0:T(8,128)} %latents.1, s32[1,136]{1,0:T(1,128)} %bitcast.19, s32[1,1024]{1,0:T(1,128)} %bitcast.15, f32[2,3072]{1,0:T(2,128)} %mod_scale.1, f32[2,3072]{1,0:T(2,128)} %mod_shift.1, f32[6,128]{1,0:T(8,128)} %bitcast.16, f32[6,128]{1,0:T(8,128)} %bitcast.17, ...), custom_call_target="tpu_custom_call" | custom-call | tf_op jit(solution)/shard_map/pallas_call | solution.py:494
  109.9 1.4 %copy.24 = bf16[2,2,8,512]{3,1,0,2:T(2,128)(2,1)} copy(bf16[2,2,8,512]{3,2,1,0:T(8,128)(2,1)} %bitcast.13) | data formatting | bytes 65536 | tf_op jit(solution)/shard_map/reshape | solution.py:564
  111.3 1.5 %copy.26 = f32[136,128]{1,0:T(8,128)} copy(f32[136,128]{1,0:T(8,128)} %get-tuple-element.8) | data formatting | bytes 139264
